TPU v7x, 128 devices: a whole 4x4x4 slice. The times are simulated.
128 devices in a mesh: dp: 32 (over x, z, core), owner: 4 (over y).
Axes of the slice: x: 4, y: 4, z: 4, core: 2. Of those that a mesh axis runs over, the one named last changes fastest.
Arguments:
- hidden: bfloat16 [32768, 6912], P(('dp', 'owner')), may hold values from -6 to 6
- grad_out: bfloat16 [32768, 2560], P(('dp', 'owner')), may hold values from -6 to 6
- block_list: int32 [512, 2], replicated, may hold values from 0 to 107, as said below
- live_block_count: int32 [128], replicated, may hold values from 1 to 4, as said below
- master: float32 [512, 4096], P(('dp', 'owner')), may hold values from -6 to 6
- moment: float32 [512, 4096], P(('dp', 'owner')), may hold values from -6 to 6
- variance: float32 [512, 4096], P(('dp', 'owner')), may hold values from 0.25 to 4
Outputs:
- new_master: float32 [512, 4096], P(('dp', 'owner'))
- new_moment: float32 [512, 4096], P(('dp', 'owner'))
- new_variance: float32 [512, 4096], P(('dp', 'owner'))
- clipped_grad: float32 [512, 4096], P(('dp', 'owner'))
- published: bfloat16 [512, 4096], replicated
Inputs may be any that keep to these rules, and one draw needn't show every extreme that they name: `block_list`: each row names a block: its row index below 108, its column index below 40; all rows name different blocks. Rows 4 o to 4 o + 3 are owner o's slots; owner o is the device whose index along dp is o // 4 and whose index along the mesh axis `owner` is o mod 4. Owner o's first live_block_count[o] slots are live, the rest padding; some owner's slots are all live.
All inputs are finite; a program needn't handle non-finite values.
Results may differ from a plain program's by a relative error of at most 0.001.
Values may be sent and summed in bfloat16 or wider, within the bound.
A program may use at most 128 MiB of HBM per device.

v0:
```python
import math
import jax
import jax.numpy as jnp
from jax import lax
from jax.sharding import PartitionSpec as P

BLOCK_SIDE_SIZE = 64
OWNER_SLOTS = 4


def block_terms(hidden, grad_out, row_indices, column_indices, active_slot_mask, row_count):
    tok_rows = hidden.shape[0]
    block_side = BLOCK_SIDE_SIZE
    group_size = math.gcd(row_count, 8 * OWNER_SLOTS)
    hidden_blocks = hidden.reshape(tok_rows, hidden.shape[1] // block_side, block_side)
    output_blocks = grad_out.reshape(tok_rows, grad_out.shape[1] // block_side, block_side)

    def one_group(id_pair):
        row_sel, col_sel = id_pair
        left_cols = jnp.take(hidden_blocks, row_sel, axis=1)
        right_cols = jnp.take(output_blocks, col_sel, axis=1)
        products = lax.dot_general(
            left_cols, right_cols, (((0,), (0,)), ((1,), (1,))), preferred_element_type=jnp.float32
        )
        return products.reshape(group_size, block_side * block_side)

    group_terms = lax.map(
        one_group, (row_indices.reshape(-1, group_size), column_indices.reshape(-1, group_size))
    )
    group_terms = group_terms.reshape(row_count, block_side * block_side)
    return jnp.where(active_slot_mask[:, None], group_terms, jnp.zeros_like(group_terms))


def local(hidden, grad_out, block_list, live_block_count, master, moment, variance):
    slot_rows = master.shape[0]
    row_indices = block_list[:, 0]
    column_indices = block_list[:, 1]
    active_slot_mask = (
        jnp.arange(slot_rows, dtype=jnp.int32)[None, :] < live_block_count[:, None]
    ).reshape(-1)
    weight_gradient = lax.psum_scatter(
        block_terms(
            hidden,
            grad_out,
            row_indices,
            column_indices,
            active_slot_mask,
            lax.axis_size(("dp", "owner")) * slot_rows,
        ),
        ("dp", "owner"),
        scatter_dimension=0,
        tiled=True,
    )
    square_total = lax.psum(jnp.sum(weight_gradient * weight_gradient), ("dp", "owner"))
    live_total = jnp.sum(live_block_count).astype(jnp.float32) * weight_gradient.shape[1]
    mean_square = square_total / live_total
    clip_scale = jnp.minimum(1.0, 1.0 / jnp.sqrt(mean_square + 1e-06))
    clipped_grad = clip_scale * weight_gradient
    new_moment = 0.9 * moment + 0.1 * clipped_grad
    new_variance = 0.95 * variance + 0.05 * clipped_grad * clipped_grad
    moment_hat = new_moment / (1.0 - 0.9**20)
    variance_hat = new_variance / (1.0 - 0.95**20)
    new_master = master - 0.02 * (moment_hat / (jnp.sqrt(variance_hat) + 1e-08) + 0.1 * master)
    own_blocks = new_master.astype(jnp.bfloat16)
    published = lax.all_gather(own_blocks, ("dp", "owner"), axis=0, tiled=True)
    return (new_master, new_moment, new_variance, clipped_grad, published)


def solution(mesh):
    return jax.shard_map(
        local,
        mesh=mesh,
        in_specs=(
            P(("dp", "owner"), None),
            P(("dp", "owner"), None),
            P(),
            P(),
            P(("dp", "owner"), None),
            P(("dp", "owner"), None),
            P(("dp", "owner"), None),
        ),
        out_specs=(
            P(("dp", "owner"), None),
            P(("dp", "owner"), None),
            P(("dp", "owner"), None),
            P(("dp", "owner"), None),
            P(),
        ),
        check_vma=False,
    )
```

profile of v0, /device:TPU:1, one launch (start us, length us, event | category | flops | bytes accessed | tf_op | source)
XLA Modules:
  0.0 451.4 jit_solution(7616821432423559366)
XLA Ops:
  8.2 6.0 %copy.16 = bf16[256,6912]{0,1:T(8,128)(2,1)} copy(bf16[256,6912]{1,0:T(8,128)(2,1)} %param.9) | data formatting | bytes 7077888 | tf_op args[0]
  14.1 1.6 copy.17
  15.7 115.8 %while.10 = (s32[]{:T(128)}, f32[16,32,4096]{2,1,0:T(8,128)}, s32[16,32]{1,0:T(8,128)S(1)}, bf16[256,108,64]{0,2,1:T(8,128)(2,1)}, s32[16,32]{1,0:T(8,128)S(1)}, /*index=5*/bf16[256,40,64]{0,2,1:T(8,128)(2,1)S(1)}, s32[]{:T(128)}) while((s32[]{:T(128)}, f32[16,32,4096]{2,1,0:T(8,128)}, s32[16,32]{1,0:T(8,128)S(1)}, ...), condition=%wide.region_1.2_spmd, body=%wide.region_0.1_spmd.sunk | while | flops 68160064 | bytes 8923093 | solution.py:27
  16.4 2.6 gather_fusion.1
  20.6 1.6 broadcast_in_dim.44
  23.7 2.6 gather_fusion.1
  27.8 1.6 broadcast_in_dim.44
  31.0 2.6 gather_fusion.1
  35.1 1.6 broadcast_in_dim.44
  38.2 2.6 gather_fusion.1
  42.4 1.6 broadcast_in_dim.44
  45.4 2.6 gather_fusion.1
  52.7 2.6 gather_fusion.1
  59.9 2.6 gather_fusion.1
  67.1 2.6 gather_fusion.1
  74.4 2.6 gather_fusion.1
  78.5 1.6 broadcast_in_dim.44
  81.6 2.6 gather_fusion.1
  85.8 1.6 broadcast_in_dim.44
  88.9 2.6 gather_fusion.1
  96.1 2.6 gather_fusion.1
  103.3 2.6 gather_fusion.1
  110.5 2.6 gather_fusion.1
  117.8 2.6 gather_fusion.1
  121.9 1.6 broadcast_in_dim.44
  125.0 2.6 gather_fusion.1
  131.8 8.2 %bitcast_select_fusion = f32[512,4096]{1,0:T(8,128)} fusion(f32[16,32,4096]{2,1,0:T(8,128)} %get-tuple-element.37, pred[512]{0:T(512)(128)(4,1)S(1)} %lt.64), kind=kLoop, calls=%fused_computation.24 | loop fusion | flops 2097152 | bytes 16777728 | tf_op jit(solution)/shard_map/jit(_where)/select_n | solution.py:31
  141.4 163.7 %all-reduce.3.cloned.1.call-done = f32[512,4096]{1,0:T(8,128)} async-done(((f32[512,4096]{1,0:T(8,128)}), f32[512,4096]{1,0:T(8,128)}) %all-reduce.3.cloned.1.call-update) | async-done | bytes 8388624
  306.7 64.0 %psum.7 = f32[]{:T(128)} all-reduce(f32[]{:T(128)} %multiply_reduce_fusion), channel_id=1, replica_groups=mesh['dp'=32,'owner'=4] {'dp','owner'}, use_global_device_ids=true, to_apply=%region_4.5 | all-reduce | flops 1 | bytes 8 | tf_op jit(solution)/shard_map/psum | solution.py:54
  371.4 1.7 convert_bitcast_fusion
  373.1 64.5 %all-gather.3.cloned.1.call-done = bf16[128,4,4096]{2,1,0:T(4,128)(2,1)} async-done(((bf16[1,4,4096]{2,1,0:T(4,128)(2,1)}), bf16[128,4,4096]{2,1,0:T(4,128)(2,1)}) %all-gather.3.cloned.1.call-update) | async-done | bytes 4194320 | tf_op jit(solution)/shard_map/all_gather | solution.py:65
  437.7 6.9 %reshape.124 = bf16[512,4096]{1,0:T(8,128)(2,1)} reshape(bf16[128,4,4096]{2,1,0:T(4,128)(2,1)} %all-gather.3.cloned.1.call-done) | data formatting | bytes 8388608
  (141 shorter events, 65.8 us)
Async XLA Ops:
  7.2 298.0 %all-reduce.3.cloned.1.call-start = ((), (), s32[]{:S(2)}) async-start(), calls=%async_computation.1 | async-start | bytes 16777216
  15.7 115.8 %copy-start.3 = (s32[128]{0:T(128)S(1)}, s32[128]{0:T(128)}, u32[]{:S(2)}) copy-start(s32[128]{0:T(128)} %param.12) | copy-start | bytes 1540
  140.0 231.4 %copy-start = (f32[4,4096]{1,0:T(4,128)S(1)}, f32[4,4096]{1,0:T(4,128)}, u32[]{:S(2)}) copy-start(f32[4,4096]{1,0:T(4,128)} %param.13) | copy-start | bytes 196612
  140.0 231.4 %copy-start.1 = (f32[4,4096]{1,0:T(4,128)S(1)}, f32[4,4096]{1,0:T(4,128)}, u32[]{:S(2)}) copy-start(f32[4,4096]{1,0:T(4,128)} %param.14) | copy-start | bytes 196612
  140.0 231.4 %copy-start.2 = (f32[4,4096]{1,0:T(4,128)S(1)}, f32[4,4096]{1,0:T(4,128)}, u32[]{:S(2)}) copy-start(f32[4,4096]{1,0:T(4,128)} %param.15) | copy-start | bytes 196612
  140.0 297.6 %all-gather.3.cloned.1.call-start = ((), (), s32[]{:S(2)}) async-start(), calls=%async_computation | async-start | bytes 4227072 | tf_op jit(solution)/shard_map/all_gather | solution.py:65
Sparse Core Ops, SparseCore 0:
  140.2 164.9 all-reduce.2
  373.3 64.3 all-gather.2
where the time goes:
time: 453 us; the launch traced here: 451 us
  waiting for transfers between devices  228 us (50%)
  local copies, waits for them, and re-layouts  106 us (23%)
  blocking collectives  64 us (14%)
  matrix products  24 us (5%)
  between operations  15.5 us (3%)
  other arithmetic  12.8 us (3%)
    unnamed x3, waiting for transfers between devices  164 us
    all_gather x1, waiting for transfers between devices, local(): published = lax.all_gather(own_blocks, ('dp', 'owner'), axis=0, tiled=True)  64.5 us
    psum x1, blocking collectives, local(): lax.psum(jnp.sum(weight_gradient * weight_gradient), ('dp', 'owner'))  64 us
    gather x16, local copies, waits for them, and re-layouts, one_group(): left_cols = jnp.take(hidden_blocks, row_sel, axis=1)  41.9 us
    broadcast_in_dim x16, local copies, waits for them, and re-layouts, block_terms(): lax.map(one_group, (row_indices.reshape(-1, group_size), column_indices.r...  25.3 us
    dot_general x16, matrix products, one_group(): lax.dot_general(left_cols, right_cols, (((0,), (0,)), ((1,), (1,))), pref...  24 us
    unnamed x11, local copies, waits for them, and re-layouts  14.5 us
    dynamic_update_slice x16, local copies, waits for them, and re-layouts, block_terms(): lax.map(one_group, (row_indices.reshape(-1, group_size), column_indices.r...  13.6 us
  transfers between devices with their start and end apart: 2, of which 2 were waited for; matrix products, arithmetic and copies ran while one was open for 0% of the time, Pallas kernels for 0%

commit v1 on v0

--- a/solution.py
+++ b/solution.py
@@ -62,7 +62,10 @@
     variance_hat = new_variance / (1.0 - 0.95**20)
     new_master = master - 0.02 * (moment_hat / (jnp.sqrt(variance_hat) + 1e-08) + 0.1 * master)
     own_blocks = new_master.astype(jnp.bfloat16)
-    published = lax.all_gather(own_blocks, ("dp", "owner"), axis=0, tiled=True)
+    count = lax.axis_size(("dp", "owner"))
+    blocks = jnp.stack([own_blocks for _ in range(count)])
+    blocks = lax.all_to_all(blocks, ("dp", "owner"), split_axis=0, concat_axis=0)
+    published = jnp.concatenate(blocks, axis=0)
     return (new_master, new_moment, new_variance, clipped_grad, published)
 
 

time: 453 us -> 449 us (level)
  waiting for transfers between devices: 228 us -> 164 us
  blocking collectives: 64 us -> 123 us
    all_gather x1 -> x0, waiting for transfers between devices: 64.5 us -> none  [local(): published = lax.all_gather(own_blocks, ('dp', 'owner'), axis=0, tiled=True)]
    all_to_all x0 -> x1, blocking collectives: none -> 58.7 us  [local(): lax.all_to_all(blocks, ('dp', 'owner'), split_axis=0, concat_axis=0)]
    reshape x0 -> x1, local copies, waits for them, and re-layouts: none -> 6.87 us  [local(): published = jnp.concatenate(blocks, axis=0)]
    unnamed x11 -> x10, local copies, waits for them, and re-layouts: 14.5 us -> 7.59 us
    unnamed x3 -> x2, waiting for transfers between devices: 164 us -> 164 us
  transfers between devices with their start and end apart: 2 -> 1, of which waited for: 2 -> 1; matrix products, arithmetic and copies ran while one was open for 0% -> 0% of each run, Pallas kernels for 0% -> 0%
where the time goes in v1:
time: 449 us; the launch traced here: 448 us
  waiting for transfers between devices  164 us (37%)
  blocking collectives  123 us (27%)
  local copies, waits for them, and re-layouts  108 us (24%)
  matrix products  24 us (5%)
  between operations  15.5 us (3%)
  other arithmetic  12.8 us (3%)
    unnamed x2, waiting for transfers between devices  164 us
    psum x1, blocking collectives, local(): lax.psum(jnp.sum(weight_gradient * weight_gradient), ('dp', 'owner'))  64 us
    all_to_all x1, blocking collectives, local(): lax.all_to_all(blocks, ('dp', 'owner'), split_axis=0, concat_axis=0)  58.7 us
    gather x16, local copies, waits for them, and re-layouts, one_group(): left_cols = jnp.take(hidden_blocks, row_sel, axis=1)  41.9 us
    broadcast_in_dim x16, local copies, waits for them, and re-layouts, block_terms(): lax.map(one_group, (row_indices.reshape(-1, group_size), column_indices.r...  25.3 us
    dot_general x16, matrix products, one_group(): lax.dot_general(left_cols, right_cols, (((0,), (0,)), ((1,), (1,))), pref...  24 us
    dynamic_update_slice x16, local copies, waits for them, and re-layouts, block_terms(): lax.map(one_group, (row_indices.reshape(-1, group_size), column_indices.r...  13.6 us
    gather x16, local copies, waits for them, and re-layouts, one_group(): right_cols = jnp.take(output_blocks, col_sel, axis=1)  9.82 us
  transfers between devices with their start and end apart: 1, of which 1 were waited for; matrix products, arithmetic and copies ran while one was open for 0% of the time, Pallas kernels for 0%

profile of v1, /device:TPU:1, one launch (start us, length us, event | category | flops | bytes accessed | tf_op | source)
XLA Modules:
  0.0 447.6 jit_solution(15638497430426440236)
XLA Ops:
  8.2 6.0 %copy.16 = bf16[256,6912]{0,1:T(8,128)(2,1)} copy(bf16[256,6912]{1,0:T(8,128)(2,1)} %param.9) | data formatting | bytes 7077888 | tf_op args[0]
  14.1 1.6 copy.17
  15.7 115.8 %while.10 = (s32[]{:T(128)}, f32[16,32,4096]{2,1,0:T(8,128)}, s32[16,32]{1,0:T(8,128)S(1)}, bf16[256,108,64]{0,2,1:T(8,128)(2,1)}, s32[16,32]{1,0:T(8,128)S(1)}, /*index=5*/bf16[256,40,64]{0,2,1:T(8,128)(2,1)S(1)}, s32[]{:T(128)}) while((s32[]{:T(128)}, f32[16,32,4096]{2,1,0:T(8,128)}, s32[16,32]{1,0:T(8,128)S(1)}, ...), condition=%wide.region_1.2_spmd, body=%wide.region_0.1_spmd.sunk | while | flops 68160064 | bytes 8923093 | solution.py:27
  16.4 2.6 gather_fusion.1
  20.6 1.6 broadcast_in_dim.44
  23.7 2.6 gather_fusion.1
  31.0 2.6 gather_fusion.1
  35.1 1.6 broadcast_in_dim.44
  38.2 2.6 gather_fusion.1
  42.4 1.6 broadcast_in_dim.44
  45.4 2.6 gather_fusion.1
  52.7 2.6 gather_fusion.1
  59.9 2.6 gather_fusion.1
  67.1 2.6 gather_fusion.1
  74.4 2.6 gather_fusion.1
  78.5 1.6 broadcast_in_dim.44
  81.6 2.6 gather_fusion.1
  85.8 1.6 broadcast_in_dim.44
  88.9 2.6 gather_fusion.1
  96.1 2.6 gather_fusion.1
  103.3 2.6 gather_fusion.1
  110.5 2.6 gather_fusion.1
  117.8 2.6 gather_fusion.1
  121.9 1.6 broadcast_in_dim.44
  125.0 2.6 gather_fusion.1
  131.8 8.2 %bitcast_select_fusion = f32[512,4096]{1,0:T(8,128)} fusion(f32[16,32,4096]{2,1,0:T(8,128)} %get-tuple-element.37, pred[512]{0:T(512)(128)(4,1)S(1)} %lt.64), kind=kLoop, calls=%fused_computation.24 | loop fusion | flops 2097152 | bytes 16777728 | tf_op jit(solution)/shard_map/jit(_where)/select_n | solution.py:31
  141.3 163.8 %all-reduce.3.cloned.1.call-done = f32[512,4096]{1,0:T(8,128)} async-done(((f32[512,4096]{1,0:T(8,128)}), f32[512,4096]{1,0:T(8,128)}) %all-reduce.3.cloned.1.call-update) | async-done | bytes 8388624
  306.7 64.0 %psum.7 = f32[]{:T(128)} all-reduce(f32[]{:T(128)} %multiply_reduce_fusion), channel_id=1, replica_groups=mesh['dp'=32,'owner'=4] {'dp','owner'}, use_global_device_ids=true, to_apply=%region_4.5 | all-reduce | flops 1 | bytes 8 | tf_op jit(solution)/shard_map/psum | solution.py:54
  371.4 1.7 fusion.12
  373.1 2.1 stack.2
  375.2 58.7 %all_to_all.5 = bf16[128,4,4096]{2,1,0:T(4,128)(2,1)} all-to-all(bf16[128,4,4096]{2,1,0:T(4,128)(2,1)S(1)} %stack.2), channel_id=1, replica_groups=mesh['dp'=32,'owner'=4] {'dp','owner'}, dimensions={0} | all-to-all | bytes 8388608 | tf_op jit(solution)/shard_map/all_to_all | solution.py:67
  433.9 6.9 %reshape.112 = bf16[512,4096]{1,0:T(8,128)(2,1)} reshape(bf16[128,4,4096]{2,1,0:T(4,128)(2,1)} %all_to_all.5) | data formatting | bytes 8388608 | tf_op jit(solution)/shard_map/reshape | solution.py:68
  (140 shorter events, 67.3 us)
Async XLA Ops:
  7.2 298.0 %all-reduce.3.cloned.1.call-start = ((), (), s32[]{:S(2)}) async-start(), calls=%async_computation.1 | async-start | bytes 16777216
  15.7 115.8 %copy-start.3 = (s32[128]{0:T(128)S(1)}, s32[128]{0:T(128)}, u32[]{:S(2)}) copy-start(s32[128]{0:T(128)} %param.12) | copy-start | bytes 1540
  140.0 231.4 %copy-start = (f32[4,4096]{1,0:T(4,128)S(1)}, f32[4,4096]{1,0:T(4,128)}, u32[]{:S(2)}) copy-start(f32[4,4096]{1,0:T(4,128)} %param.13) | copy-start | bytes 196612
  140.0 231.4 %copy-start.1 = (f32[4,4096]{1,0:T(4,128)S(1)}, f32[4,4096]{1,0:T(4,128)}, u32[]{:S(2)}) copy-start(f32[4,4096]{1,0:T(4,128)} %param.14) | copy-start | bytes 196612
  140.0 231.4 %copy-start.2 = (f32[4,4096]{1,0:T(4,128)S(1)}, f32[4,4096]{1,0:T(4,128)}, u32[]{:S(2)}) copy-start(f32[4,4096]{1,0:T(4,128)} %param.15) | copy-start | bytes 196612
Sparse Core Ops, SparseCore 0:
  140.2 164.9 all-reduce.2
